TPU v7x, 128 devices: a whole 4x4x4 slice. The times are simulated.
128 devices in a mesh: gx: 4 (over y_hi, core), gy: 4 (over x), gz: 8 (over z, y_lo).
Axes of the slice: x: 4, y: 4 (y_hi: 2, y_lo: 2; y = y_hi * 2 + y_lo), z: 4, core: 2. Of those that a mesh axis runs over, the one named last changes fastest.
Arguments:
- terminal_adjoint: float32 [19, 64, 128, 1024], P(None, 'gx', 'gy', 'gz'), may hold values from -6 to 6
- saved_velocity: float32 [4, 3, 64, 128, 1024], P(None, None, 'gx', 'gy', 'gz'), may hold values from -0.15 to 0.15
- solid_mask: int32 [64, 128, 1024], P('gx', 'gy', 'gz'), may hold values 0 or 1
- wall_ids: int32 [64, 128, 1024], P('gx', 'gy', 'gz'), may hold values from 0 to 255
Outputs:
- adjoint_out: float32 [19, 64, 128, 1024], P(None, 'gx', 'gy', 'gz')
- wall_grad: float32 [4, 128], replicated
Inputs may be any that keep to these rules, and one draw needn't show every extreme that they name: `wall_ids`: ids of 128 or more mark cells on no wall panel.
All inputs are finite; a program needn't handle non-finite values. No bound on the sum of `solid_mask` on one device may be relied on, other than what follows from the above.
Results may differ from a plain program's by a relative error of at most 0.0003.
Values sent between devices are 32-bit elements; how exact they have to be, the bound alone decides.
A program may use at most 128 MiB of HBM per device.

v0:
```python
import functools

import jax
import jax.numpy as jnp
from jax import lax
from jax.experimental import pallas as pl
from jax.experimental.pallas import tpu as pltpu
from jax.sharding import PartitionSpec as P

STEPS = 4
WALLS = 128
OMEGA = 1.25
LATTICE = (
    (0, 0, 0),
    (1, 0, 0),
    (-1, 0, 0),
    (0, 1, 0),
    (0, -1, 0),
    (0, 0, 1),
    (0, 0, -1),
    (1, 1, 0),
    (-1, -1, 0),
    (1, -1, 0),
    (-1, 1, 0),
    (1, 0, 1),
    (-1, 0, -1),
    (1, 0, -1),
    (-1, 0, 1),
    (0, 1, 1),
    (0, -1, -1),
    (0, 1, -1),
    (0, -1, 1),
)
OPPOSITE = (0, 2, 1, 4, 3, 6, 5, 8, 7, 10, 9, 12, 11, 14, 13, 16, 15, 18, 17)

NX, NY, NZ = 16, 32, 128
ROW0 = 8
ROWS = 48
GROUPS = NY // 8

SLOT = {9: 16, 1: 1, 11: 2, 13: 3, 7: 4, 3: 5, 15: 6, 17: 7, 10: 8, 2: 9,
        12: 10, 14: 11, 8: 12, 4: 13, 16: 14, 18: 15, 5: 17, 6: 18, 0: 19}
SLOTS = 20
Y_MEMBERS = ((7, 3, 15, 17, 10), (8, 4, 16, 18, 9))
Z_MEMBERS = ((5, 11, 14, 15, 18), (6, 12, 13, 16, 17))
LANES = NX + 2
MESH = pl.DeviceIdType.MESH


def kernel(
    sizes, adj_ref, vel_ref, solid_ref, ids_ref, out_ref, wall_ref,
    state, vel, solid, ids, ysend, yrecv, zsend, zrecv, xyrecv, xzrecv, yzrecv,
    lo_hot, hi_part, acc, in_sem, out_sem, send_sem, recv_sem,
):
    me = (lax.axis_index("gx"), lax.axis_index("gy"), lax.axis_index("gz"))

    loads = []
    for m in range(19):
        loads.append(
            pltpu.make_async_copy(
                adj_ref.at[m],
                state.at[0, SLOT[m], pl.ds(1, NX), pl.ds(ROW0, NY), :],
                in_sem.at[m],
            )
        )
    loads.append(pltpu.make_async_copy(ids_ref, ids, in_sem.at[19]))
    loads.append(pltpu.make_async_copy(solid_ref, solid, in_sem.at[20]))
    loads.append(pltpu.make_async_copy(vel_ref, vel, in_sem.at[21]))
    for load in loads:
        load.start()

    zero_plane = jnp.zeros((SLOTS, ROWS, NZ), jnp.float32)
    for b in range(2):
        state[b, :, 0] = zero_plane
        state[b, :, NX + 1] = zero_plane
    yrecv[...] = jnp.zeros_like(yrecv)
    zrecv[...] = jnp.zeros_like(zrecv)
    xyrecv[...] = jnp.zeros_like(xyrecv)
    xzrecv[...] = jnp.zeros_like(xzrecv)
    yzrecv[...] = jnp.zeros_like(yzrecv)

    def beside(vector, sign):
        at = tuple(me[k] + sign * vector[k] for k in range(3))
        inside = None
        for k in range(3):
            if vector[k] != 0:
                here = (at[k] >= 0) & (at[k] < sizes[k])
                inside = here if inside is None else inside & here
        return at, inside

    barrier = pltpu.get_barrier_semaphore()
    count = jnp.int32(0)
    for m in range(1, 19):
        at, inside = beside(LATTICE[m], 1)
        count = count + inside.astype(jnp.int32)

        @pl.when(inside)
        def _():
            pl.semaphore_signal(barrier, inc=1, device_id=at, device_id_type=MESH)

    pl.semaphore_wait(barrier, count)

    lane = lax.broadcasted_iota(jnp.int32, (8, NZ), 1)

    def rows_of(group, shift=0):
        return pl.ds(ROW0 + 8 * group + shift, 8)

    loads[19].wait()
    low_iota = lax.broadcasted_iota(jnp.int32, (16, NZ), 0)

    def hot_plane(x, carry):
        for group in range(GROUPS):
            low = ids[x, pl.ds(8 * group, 8), :] & 15
            for y in range(8):
                hot = jnp.broadcast_to(low[y : y + 1, :], (16, NZ)) == low_iota
                lo_hot[x, pl.ds(16 * y, 16), pl.ds(NZ * group, NZ)] = jnp.where(
                    hot, 1.0, 0.0
                ).astype(jnp.bfloat16)
        return carry

    lax.fori_loop(0, NX, hot_plane, 0)

    def pack(b, x, group, values):
        for side in range(2):
            rows = pl.ds(8 * group, 8)
            packed = zsend[b, side, rows, :]
            for i, m in enumerate(Z_MEMBERS[side]):
                place = i * LANES + x + 1
                moved = pltpu.roll(values[m], place + side, 1)
                packed = jnp.where(lane == place, moved, packed)
            zsend[b, side, rows, :] = packed
        if group == 0:
            for i, m in enumerate(Y_MEMBERS[0]):
                ysend[b, 0, i, pl.ds(x, 1), :] = values[m][0:1, :]
        if group == GROUPS - 1:
            for i, m in enumerate(Y_MEMBERS[1]):
                ysend[b, 1, i, pl.ds(x, 1), :] = values[m][7:8, :]

    for m in range(19):
        loads[m].wait()

    def first_pack(x, carry):
        for group in range(GROUPS):
            values = {}
            for m in sorted(set(Y_MEMBERS[0] + Y_MEMBERS[1] + Z_MEMBERS[0] + Z_MEMBERS[1])):
                values[m] = state[0, SLOT[m], x + 1, rows_of(group), :]
            pack(0, x, group, values)
        return carry

    lax.fori_loop(0, NX, first_pack, 0)
    state[0, 0, 1, pl.ds(ROW0, NY), :] = state[0, SLOT[9], 1, pl.ds(ROW0, NY), :]
    loads[20].wait()
    loads[21].wait()

    def message(b, m):
        cells = pl.ds(ROW0, NY)
        if m == 1:
            return state.at[b, pl.ds(0, 5), 1, cells, :], state.at[b, pl.ds(0, 5), NX + 1, cells, :]
        if m == 2:
            return state.at[b, pl.ds(8, 5), NX, cells, :], state.at[b, pl.ds(8, 5), 0, cells, :]
        if m in (3, 4):
            return ysend.at[b, m - 3], yrecv.at[b, m - 3]
        if m in (5, 6):
            return zsend.at[b, m - 5], zrecv.at[b, m - 5, cells, :]
        vector = LATTICE[m]
        if m <= 10:
            side = 0 if vector[1] > 0 else 1
            start = 0 if vector[0] > 0 else NX - 8
            member = Y_MEMBERS[side].index(m)
            return ysend.at[b, side, member, pl.ds(start, 8), :], xyrecv.at[b, m - 7]
        side = 0 if vector[2] > 0 else 1
        if m <= 14:
            return zsend.at[b, side], xzrecv.at[b, m - 11]
        start = 0 if vector[1] > 0 else NY - 8
        return zsend.at[b, side, pl.ds(start, 8), :], yzrecv.at[b, m - 15]

    def copy_of(t, b, m, target):
        source, landing = message(b, m)
        return pltpu.make_async_remote_copy(
            src_ref=source,
            dst_ref=landing,
            send_sem=send_sem.at[t, m - 1],
            recv_sem=recv_sem.at[t, m - 1],
            device_id=target,
            device_id_type=MESH,
        )

    def exchange(t, b):
        for m in range(1, 19):
            at, inside = beside(LATTICE[m], -1)

            @pl.when(inside)
            def _():
                copy_of(t, b, m, at).start()

        for m in range(1, 19):
            at, inside = beside(LATTICE[m], 1)

            @pl.when(inside)
            def _():
                copy_of(t, b, m, at).wait_recv()

        for m in range(1, 19):
            at, inside = beside(LATTICE[m], -1)

            @pl.when(inside)
            def _():
                copy_of(t, b, m, at).wait_send()

    def unpack(b):
        state[b, SLOT[9], NX + 1, pl.ds(ROW0, NY), :] = state[b, 0, NX + 1, pl.ds(ROW0, NY), :]
        for side in range(2):
            row = ROW0 + NY if side == 0 else ROW0 - 1
            for i, m in enumerate(Y_MEMBERS[side]):
                for x in range(NX):
                    state[b, SLOT[m], x + 1, pl.ds(row, 1), :] = yrecv[b, side, i, pl.ds(x, 1), :]
        for m in range(7, 11):
            vector = LATTICE[m]
            plane = NX + 1 if vector[0] > 0 else 0
            row = ROW0 + NY if vector[1] > 0 else ROW0 - 1
            source = 0 if vector[0] > 0 else 7
            state[b, SLOT[m], plane, pl.ds(row, 1), :] = xyrecv[b, m - 7, pl.ds(source, 1), :]
        for m in range(11, 15):
            vector = LATTICE[m]
            side = 0 if vector[2] > 0 else 1
            i = Z_MEMBERS[side].index(m)
            source = i * LANES + (1 if vector[0] > 0 else NX)
            place = i * LANES + (NX + 1 if vector[0] > 0 else 0)
            for group in range(GROUPS):
                moved = pltpu.roll(
                    xzrecv[b, m - 11, pl.ds(8 * group, 8), :], (place - source) % NZ, 1
                )
                zrecv[b, side, rows_of(group), :] = jnp.where(
                    lane == place, moved, zrecv[b, side, rows_of(group), :]
                )
        for m in range(15, 19):
            vector = LATTICE[m]
            side = 0 if vector[2] > 0 else 1
            row = ROW0 + NY if vector[1] > 0 else ROW0 - 1
            source = 0 if vector[1] > 0 else 7
            zrecv[b, side, pl.ds(row, 1), :] = yzrecv[b, m - 15, pl.ds(source, 1), :]

    def pull(b, x, group):
        read = []
        for m in range(19):
            vector = LATTICE[m]
            value = state[b, SLOT[m], x + 1 + vector[0], rows_of(group, vector[1]), :]
            if vector[2] != 0:
                side = 0 if vector[2] > 0 else 1
                place = Z_MEMBERS[side].index(m) * LANES + x + 1 + vector[0]
                column = zrecv[b, side, rows_of(group, vector[1]), :]
                if side == 0:
                    value = jnp.where(
                        lane == NZ - 1,
                        pltpu.roll(column, NZ - 1 - place, 1),
                        pltpu.roll(value, NZ - 1, 1),
                    )
                else:
                    value = jnp.where(
                        lane == 0,
                        pltpu.roll(column, NZ - place, 1),
                        pltpu.roll(value, 1, 1),
                    )
            read.append(value)
        return read

    def collide(read, u, is_solid):
        face_sum = [read[1] + read[2], read[3] + read[4], read[5] + read[6]]
        face_dif = [read[1] - read[2], read[3] - read[4], read[5] - read[6]]
        sums, twist, first, second = [], [], [], []
        for m in (7, 11, 15):
            plus, minus = read[m] + read[m + 1], read[m + 2] + read[m + 3]
            dplus, dminus = read[m] - read[m + 1], read[m + 2] - read[m + 3]
            sums.append(plus + minus)
            twist.append(plus - minus)
            first.append(dplus + dminus)
            second.append(dplus - dminus)
        xy, xz, yz = 0, 1, 2
        twice = [value + value for value in face_sum]
        rho = 12.0 * read[0] + (twice[0] + twice[1] + twice[2]) + (sums[xy] + sums[xz] + sums[yz])
        edge = [first[xy] + first[xz], second[xy] + first[yz], second[xz] + second[yz]]
        flux = [(face_dif[k] + face_dif[k]) + edge[k] for k in range(3)]
        stress = [
            twice[0] + (sums[xy] + sums[xz]),
            twice[1] + (sums[xy] + sums[yz]),
            twice[2] + (sums[xz] + sums[yz]),
        ]
        u3 = [3.0 * value for value in u]
        w = [
            rho * u[0] - (stress[0] * u3[0] + twist[xy] * u3[1] + twist[xz] * u3[2]),
            rho * u[1] - (twist[xy] * u3[0] + stress[1] * u3[1] + twist[yz] * u3[2]),
            rho * u[2] - (twist[xz] * u3[0] + twist[yz] * u3[1] + stress[2] * u3[2]),
        ]
        g = [(OMEGA * 3.0 / 36.0) * (flux[k] - w[k]) for k in range(3)]
        base = (OMEGA / 36.0) * rho + (OMEGA * 1.5 / 36.0) * (u[0] * w[0] + u[1] * w[1] + u[2] * w[2])
        along = [None] * 19
        along[0] = base
        for k in range(3):
            along[1 + 2 * k] = base + g[k]
            along[2 + 2 * k] = base - g[k]
        for m, (j, k) in ((7, (0, 1)), (11, (0, 2)), (15, (1, 2))):
            total, difference = g[j] + g[k], g[j] - g[k]
            along[m], along[m + 1] = base + total, base - total
            along[m + 2], along[m + 3] = base + difference, base - difference
        outputs = [
            jnp.where(is_solid, read[OPPOSITE[m]], along[m] + (1.0 - OMEGA) * read[m])
            for m in range(19)
        ]
        momentum = face_dif[2] + edge[2]
        pressure = jnp.where(is_solid, -momentum, 10.0 * g[2] + (1.0 - OMEGA) * momentum)
        return outputs, pressure

    out_row = lax.broadcasted_iota(jnp.int32, (128, NZ), 0)
    out_lane = lax.broadcasted_iota(jnp.int32, (128, NZ), 1)
    same_y = (out_row & 7) == (out_lane >> 4)
    own_lane = lax.broadcasted_iota(jnp.int32, (8, NZ), 0) == (lane >> 4)

    def one_step(t, carry):
        b = lax.rem(t, 2)
        nb = 1 - b
        exchange(t, b)
        unpack(b)
        acc[...] = jnp.zeros_like(acc)

        def one_plane(x, inner):
            for group in range(GROUPS):
                rows = pl.ds(8 * group, 8)
                read = pull(b, x, group)
                u = [vel[STEPS - 1 - t, k, x, rows, :] for k in range(3)]
                outputs, pressure = collide(read, u, solid[x, rows, :] == 1)
                for m in range(19):
                    state[nb, SLOT[m], x + 1, rows_of(group), :] = outputs[m]
                pack(nb, x, group, outputs)
                upper = pressure.astype(jnp.bfloat16).astype(jnp.float32)
                both = jnp.concatenate([upper, pressure - upper], axis=0).astype(jnp.bfloat16)
                high = (ids[x, rows, :] >> 4).astype(jnp.float32)
                high = jnp.concatenate([high, high], axis=0).astype(jnp.bfloat16)
                for h in range(8):
                    hi_part[pl.ds(16 * h, 16), pl.ds(NZ * group, NZ)] = jnp.where(
                        high == h, both, jnp.zeros_like(both)
                    )
            acc[...] += lax.dot_general(
                hi_part[...],
                lo_hot[x],
                (((1,), (1,)), ((), ())),
                preferred_element_type=jnp.float32,
            )
            return inner

        lax.fori_loop(0, NX, one_plane, 0)
        state[nb, 0, 1, pl.ds(ROW0, NY), :] = state[nb, SLOT[9], 1, pl.ds(ROW0, NY), :]

        own = jnp.where(same_y, acc[...], 0.0)
        total = jnp.sum(own.reshape(8, 16, NZ), axis=1)
        for shift in (64, 32, 16):
            total = total + pltpu.roll(total, shift, 1)
        wall_ref[pl.ds(STEPS - 1 - t, 1), :] = jnp.sum(
            jnp.where(own_lane, total, 0.0), axis=0, keepdims=True
        )
        return carry

    lax.fori_loop(0, STEPS, one_step, 0)

    stores = []
    for m in range(19):
        stores.append(
            pltpu.make_async_copy(
                state.at[STEPS % 2, SLOT[m], pl.ds(1, NX), pl.ds(ROW0, NY), :],
                out_ref.at[m],
                out_sem.at[m],
            )
        )
    for store in stores:
        store.start()
    for store in stores:
        store.wait()


def body(terminal_adjoint, saved_velocity, solid_mask, wall_ids):
    sizes = tuple(lax.axis_size(name) for name in ("gx", "gy", "gz"))
    cells_all = NX * NY * NZ * sizes[0] * sizes[1] * sizes[2]
    scale = (cells_all / (2.0 * WALLS)) ** (-0.5)
    f32, vmem = jnp.float32, pltpu.VMEM
    adjoint, local = pl.pallas_call(
        functools.partial(kernel, sizes),
        out_shape=(
            jax.ShapeDtypeStruct((19, NX, NY, NZ), f32),
            jax.ShapeDtypeStruct((STEPS, WALLS), f32),
        ),
        in_specs=[pl.BlockSpec(memory_space=pl.ANY)] * 4,
        out_specs=(pl.BlockSpec(memory_space=pl.ANY), pl.BlockSpec(memory_space=pltpu.VMEM)),
        scratch_shapes=[
            vmem((2, SLOTS, NX + 2, ROWS, NZ), f32),
            vmem((STEPS, 3, NX, NY, NZ), f32),
            vmem((NX, NY, NZ), jnp.int32),
            vmem((NX, NY, NZ), jnp.int32),
            vmem((2, 2, 5, NX, NZ), f32),
            vmem((2, 2, 5, NX, NZ), f32),
            vmem((2, 2, NY, NZ), f32),
            vmem((2, 2, ROWS, NZ), f32),
            vmem((2, 4, 8, NZ), f32),
            vmem((2, 4, NY, NZ), f32),
            vmem((2, 4, 8, NZ), f32),
            vmem((NX, 128, GROUPS * NZ), jnp.bfloat16),
            vmem((128, GROUPS * NZ), jnp.bfloat16),
            vmem((128, NZ), f32),
            pltpu.SemaphoreType.DMA((22,)),
            pltpu.SemaphoreType.DMA((19,)),
            pltpu.SemaphoreType.DMA((STEPS, 18)),
            pltpu.SemaphoreType.DMA((STEPS, 18)),
        ],
        compiler_params=pltpu.CompilerParams(
            collective_id=0, has_side_effects=True, vmem_limit_bytes=48 * 2**20
        ),
        name="adjoint_steps",
    )(terminal_adjoint, saved_velocity, solid_mask, wall_ids)
    wall_grad = lax.psum(local, ("gx", "gy", "gz")) * scale
    return (adjoint, wall_grad)


def solution(mesh):
    return jax.shard_map(
        body,
        mesh=mesh,
        in_specs=(
            P(None, "gx", "gy", "gz"),
            P(None, None, "gx", "gy", "gz"),
            P("gx", "gy", "gz"),
            P("gx", "gy", "gz"),
        ),
        out_specs=(P(None, "gx", "gy", "gz"), P()),
        check_vma=False,
    )
```

profile of v0, /device:TPU:1, one launch (start us, length us, event | category | flops | bytes accessed | tf_op | source)
XLA Modules:
  0.0 148.0 jit_solution(2660588710090731585)
XLA Ops:
  0.6 0.0 copy-start
  0.6 1.9 %copy-done = f32[4,3,16,32,128]{4,3,2,1,0:T(8,128)S(1)} copy-done((f32[4,3,16,32,128]{4,3,2,1,0:T(8,128)S(1)}, f32[4,3,16,32,128]{4,3,2,1,0:T(8,128)}, u32[]{:S(2)}) %copy-start) | copy-done | bytes 3145752
  2.5 0.0 copy-start.1
  2.5 0.9 copy-done.1
  3.5 0.0 copy-start.2
  3.5 0.9 copy-done.2
  4.4 73.1 %adjoint_steps.1 = (f32[19,16,32,128]{3,2,1,0:T(8,128)}, f32[4,128]{1,0:T(4,128)S(1)}) custom-call(f32[19,16,32,128]{3,2,1,0:T(8,128)} %adj_ref.1, f32[4,3,16,32,128]{4,3,2,1,0:T(8,128)S(1)} %copy-done, s32[16,32,128]{2,1,0:T(8,128)S(1)} %copy-done.1, s32[16,32,128]{2,1,0:T(8,128)S(1)} %copy-done.2), custom_call_target="tpu_custom_call" | custom-call | tf_op jit(solution)/shard_map/adjoint_steps/pallas_call | solution.py:384
  77.5 64.5 %psum.7 = f32[4,128]{1,0:T(4,128)S(1)} all-reduce(f32[4,128]{1,0:T(4,128)S(1)} %get-tuple-element.5), channel_id=1, replica_groups=mesh['gx'=4,'gy'=4,'gz'=8] {'gx','gy','gz'}, use_global_device_ids=true, to_apply=%region_0.0 | all-reduce | flops 512 | bytes 4096 | tf_op jit(solution)/shard_map/psum | solution.py:417
  142.0 0.6 broadcast_multiply_fusion
  142.6 5.4 %copy.7 = f32[19,16,32,128]{3,2,1,0:T(8,128)} copy(f32[19,16,32,128]{3,2,1,0:T(8,128)} %get-tuple-element.8) | data formatting | bytes 9961472
Async XLA Ops:
  0.6 1.9 %copy-start = (f32[4,3,16,32,128]{4,3,2,1,0:T(8,128)S(1)}, f32[4,3,16,32,128]{4,3,2,1,0:T(8,128)}, u32[]{:S(2)}) copy-start(f32[4,3,16,32,128]{4,3,2,1,0:T(8,128)} %vel_ref.1) | copy-start | bytes 9437188
  2.5 0.9 copy-start.1
  3.5 0.9 copy-start.2
where the time goes:
time: 148 us
  Pallas kernels  73.1 us (49%)
  blocking collectives  64.5 us (44%)
  local copies, waits for them, and re-layouts  9.22 us (6%)
    pallas_call x1, Pallas kernels, body(): pl.pallas_call(functools.partial(kernel, sizes), out_shape=(jax.ShapeDtyp...  73.1 us
    psum x1, blocking collectives, body(): wall_grad = lax.psum(local, ('gx', 'gy', 'gz')) * scale  64.5 us
    unnamed x7, local copies, waits for them, and re-layouts  9.22 us

commit v1 on v0

--- a/solution.py
+++ b/solution.py
@@ -50,7 +50,8 @@
 def kernel(
     sizes, adj_ref, vel_ref, solid_ref, ids_ref, out_ref, wall_ref,
     state, vel, solid, ids, ysend, yrecv, zsend, zrecv, xyrecv, xzrecv, yzrecv,
-    lo_hot, hi_part, acc, in_sem, out_sem, send_sem, recv_sem,
+    lo_hot, hi_part, acc, sums, wall_xy, wall_z,
+    in_sem, out_sem, send_sem, recv_sem, xy_sem, z_sem,
 ):
     me = (lax.axis_index("gx"), lax.axis_index("gy"), lax.axis_index("gz"))
 
@@ -98,7 +99,16 @@
         def _():
             pl.semaphore_signal(barrier, inc=1, device_id=at, device_id_type=MESH)
 
-    pl.semaphore_wait(barrier, count)
+    plane = sizes[0] * sizes[1]
+    xy_others, z_others = [], []
+    for k in range(1, plane):
+        there = lax.rem(me[0] * sizes[1] + me[1] + k, plane)
+        xy_others.append((there // sizes[1], lax.rem(there, sizes[1]), me[2]))
+    for k in range(1, sizes[2]):
+        z_others.append((me[0], me[1], lax.rem(me[2] + k, sizes[2])))
+    for target in xy_others + z_others:
+        pl.semaphore_signal(barrier, inc=1, device_id=target, device_id_type=MESH)
+    pl.semaphore_wait(barrier, count + len(xy_others) + len(z_others))
 
     lane = lax.broadcasted_iota(jnp.int32, (8, NZ), 1)
 
@@ -315,8 +325,8 @@
     same_y = (out_row & 7) == (out_lane >> 4)
     own_lane = lax.broadcasted_iota(jnp.int32, (8, NZ), 0) == (lane >> 4)
 
-    def one_step(t, carry):
-        b = lax.rem(t, 2)
+    def one_step(t):
+        b = t % 2
         nb = 1 - b
         exchange(t, b)
         unpack(b)
@@ -354,12 +364,35 @@
         total = jnp.sum(own.reshape(8, 16, NZ), axis=1)
         for shift in (64, 32, 16):
             total = total + pltpu.roll(total, shift, 1)
-        wall_ref[pl.ds(STEPS - 1 - t, 1), :] = jnp.sum(
+        sums[pl.ds(STEPS - 1 - t, 1), :] = jnp.sum(
             jnp.where(own_lane, total, 0.0), axis=0, keepdims=True
         )
-        return carry
-
-    lax.fori_loop(0, STEPS, one_step, 0)
+
+    for t in range(STEPS):
+        one_step(t)
+
+    def gather_sum(own, slots, place, others, sems):
+        slots[place] = own
+        copies = []
+        for k, target in enumerate(others):
+            copies.append(
+                pltpu.make_async_remote_copy(
+                    src_ref=slots.at[place],
+                    dst_ref=slots.at[place],
+                    send_sem=sems.at[0, k],
+                    recv_sem=sems.at[1, k],
+                    device_id=target,
+                    device_id_type=MESH,
+                )
+            )
+        for copy in copies:
+            copy.start()
+        for copy in copies:
+            copy.wait()
+        total = slots[0]
+        for k in range(1, len(others) + 1):
+            total = total + slots[k]
+        return total
 
     stores = []
     for m in range(19):
@@ -372,22 +405,25 @@
         )
     for store in stores:
         store.start()
+    sums[pl.ds(STEPS, 8 - STEPS), :] = jnp.zeros((8 - STEPS, NZ), jnp.float32)
+    total = gather_sum(sums[...], wall_xy, me[0] * sizes[1] + me[1], xy_others, xy_sem)
+    total = gather_sum(total, wall_z, me[2], z_others, z_sem)
+    cells_all = NX * NY * NZ * sizes[0] * sizes[1] * sizes[2]
+    wall_ref[...] = total[:STEPS] * ((cells_all / (2.0 * WALLS)) ** (-0.5))
     for store in stores:
         store.wait()
 
 
 def body(terminal_adjoint, saved_velocity, solid_mask, wall_ids):
     sizes = tuple(lax.axis_size(name) for name in ("gx", "gy", "gz"))
-    cells_all = NX * NY * NZ * sizes[0] * sizes[1] * sizes[2]
-    scale = (cells_all / (2.0 * WALLS)) ** (-0.5)
     f32, vmem = jnp.float32, pltpu.VMEM
-    adjoint, local = pl.pallas_call(
+    return pl.pallas_call(
         functools.partial(kernel, sizes),
         out_shape=(
             jax.ShapeDtypeStruct((19, NX, NY, NZ), f32),
             jax.ShapeDtypeStruct((STEPS, WALLS), f32),
         ),
-        in_specs=[pl.BlockSpec(memory_space=pl.ANY)] * 4,
+        in_specs=[pl.BlockSpec(memory_space=pltpu.HBM)] * 4,
         out_specs=(pl.BlockSpec(memory_space=pl.ANY), pl.BlockSpec(memory_space=pltpu.VMEM)),
         scratch_shapes=[
             vmem((2, SLOTS, NX + 2, ROWS, NZ), f32),
@@ -404,18 +440,21 @@
             vmem((NX, 128, GROUPS * NZ), jnp.bfloat16),
             vmem((128, GROUPS * NZ), jnp.bfloat16),
             vmem((128, NZ), f32),
+            vmem((8, NZ), f32),
+            vmem((sizes[0] * sizes[1], 8, NZ), f32),
+            vmem((sizes[2], 8, NZ), f32),
             pltpu.SemaphoreType.DMA((22,)),
             pltpu.SemaphoreType.DMA((19,)),
             pltpu.SemaphoreType.DMA((STEPS, 18)),
             pltpu.SemaphoreType.DMA((STEPS, 18)),
+            pltpu.SemaphoreType.DMA((2, max(1, sizes[0] * sizes[1] - 1))),
+            pltpu.SemaphoreType.DMA((2, max(1, sizes[2] - 1))),
         ],
         compiler_params=pltpu.CompilerParams(
             collective_id=0, has_side_effects=True, vmem_limit_bytes=48 * 2**20
         ),
         name="adjoint_steps",
     )(terminal_adjoint, saved_velocity, solid_mask, wall_ids)
-    wall_grad = lax.psum(local, ("gx", "gy", "gz")) * scale
-    return (adjoint, wall_grad)
 
 
 def solution(mesh):

time: 148 us -> 75.6 us (0.51)
  blocking collectives: 64.5 us -> 0 us
  Pallas kernels: 73.1 us -> 64.9 us
    psum x1 -> x0, blocking collectives: 64.5 us -> none  [body(): wall_grad = lax.psum(local, ('gx', 'gy', 'gz')) * scale]
    pallas_call x1, Pallas kernels: 73.1 us -> 64.9 us  [body(): pl.pallas_call(functools.partial(kernel, sizes), out_shape=(jax.ShapeDtyp...]
    unnamed x7 -> x8, local copies, waits for them, and re-layouts: 9.22 us -> 9.8 us
where the time goes in v1:
time: 75.6 us; the launch traced here: 75.3 us
  Pallas kernels  64.9 us (86%)
  local copies, waits for them, and re-layouts  9.8 us (13%)
    pallas_call x1, Pallas kernels, body(): pl.pallas_call(functools.partial(kernel, sizes), out_shape=(jax.ShapeDtyp...  64.9 us
    unnamed x8, local copies, waits for them, and re-layouts  9.8 us

profile of v1, /device:TPU:1, one launch (start us, length us, event | category | flops | bytes accessed | tf_op | source)
XLA Modules:
  0.0 75.3 jit_solution(8400855552496766710)
XLA Ops:
  0.6 0.0 copy-start
  0.6 1.9 %copy-done = f32[4,3,16,32,128]{4,3,2,1,0:T(8,128)S(1)} copy-done((f32[4,3,16,32,128]{4,3,2,1,0:T(8,128)S(1)}, f32[4,3,16,32,128]{4,3,2,1,0:T(8,128)}, u32[]{:S(2)}) %copy-start) | copy-done | bytes 3145752
  2.5 0.0 copy-start.1
  2.5 0.9 %copy-done.1 = s32[16,32,128]{2,1,0:T(8,128)S(1)} copy-done((s32[16,32,128]{2,1,0:T(8,128)S(1)}, s32[16,32,128]{2,1,0:T(8,128)}, u32[]{:S(2)}) %copy-start.1) | copy-done | bytes 262168
  3.5 0.0 copy-start.2
  3.5 0.9 %copy-done.2 = s32[16,32,128]{2,1,0:T(8,128)S(1)} copy-done((s32[16,32,128]{2,1,0:T(8,128)S(1)}, s32[16,32,128]{2,1,0:T(8,128)}, u32[]{:S(2)}) %copy-start.2) | copy-done | bytes 262168
  4.4 64.9 %adjoint_steps.1 = (f32[19,16,32,128]{3,2,1,0:T(8,128)}, f32[4,128]{1,0:T(4,128)S(1)}) custom-call(f32[19,16,32,128]{3,2,1,0:T(8,128)} %adj_ref.1, f32[4,3,16,32,128]{4,3,2,1,0:T(8,128)S(1)} %copy-done, s32[16,32,128]{2,1,0:T(8,128)S(1)} %copy-done.1, s32[16,32,128]{2,1,0:T(8,128)S(1)} %copy-done.2), custom_call_target="tpu_custom_call" | custom-call | tf_op jit(solution)/shard_map/adjoint_steps/pallas_call | solution.py:420
  69.3 5.4 %copy.8 = f32[19,16,32,128]{3,2,1,0:T(8,128)} copy(f32[19,16,32,128]{3,2,1,0:T(8,128)} %get-tuple-element.4) | data formatting | bytes 9961472
  74.8 0.6 copy.9
Async XLA Ops:
  0.6 1.9 %copy-start = (f32[4,3,16,32,128]{4,3,2,1,0:T(8,128)S(1)}, f32[4,3,16,32,128]{4,3,2,1,0:T(8,128)}, u32[]{:S(2)}) copy-start(f32[4,3,16,32,128]{4,3,2,1,0:T(8,128)} %vel_ref.1) | copy-start | bytes 9437188
  2.5 0.9 %copy-start.1 = (s32[16,32,128]{2,1,0:T(8,128)S(1)}, s32[16,32,128]{2,1,0:T(8,128)}, u32[]{:S(2)}) copy-start(s32[16,32,128]{2,1,0:T(8,128)} %solid_ref.1) | copy-start | bytes 786436
  3.5 0.9 %copy-start.2 = (s32[16,32,128]{2,1,0:T(8,128)S(1)}, s32[16,32,128]{2,1,0:T(8,128)}, u32[]{:S(2)}) copy-start(s32[16,32,128]{2,1,0:T(8,128)} %ids_ref.1) | copy-start | bytes 786436

commit v2 on v1

--- a/solution.py
+++ b/solution.py
@@ -49,10 +49,11 @@
 
 def kernel(
     sizes, adj_ref, vel_ref, solid_ref, ids_ref, out_ref, wall_ref,
-    state, vel, solid, ids, ysend, yrecv, zsend, zrecv, xyrecv, xzrecv, yzrecv,
+    state0, state1, vel, solid, ids, ysend, yrecv, zsend, zrecv, xyrecv, xzrecv, yzrecv,
     lo_hot, hi_part, acc, sums, wall_xy, wall_z,
-    in_sem, out_sem, send_sem, recv_sem, xy_sem, z_sem,
+    in_sem, send_sem, recv_sem, xy_sem, z_sem,
 ):
+    state = (state0, state1)
     me = (lax.axis_index("gx"), lax.axis_index("gy"), lax.axis_index("gz"))
 
     loads = []
@@ -60,7 +61,7 @@
         loads.append(
             pltpu.make_async_copy(
                 adj_ref.at[m],
-                state.at[0, SLOT[m], pl.ds(1, NX), pl.ds(ROW0, NY), :],
+                state[0].at[SLOT[m], pl.ds(1, NX), pl.ds(ROW0, NY), :],
                 in_sem.at[m],
             )
         )
@@ -72,8 +73,8 @@
 
     zero_plane = jnp.zeros((SLOTS, ROWS, NZ), jnp.float32)
     for b in range(2):
-        state[b, :, 0] = zero_plane
-        state[b, :, NX + 1] = zero_plane
+        state[b][:, 0] = zero_plane
+        state[b][:, NX + 1] = zero_plane
     yrecv[...] = jnp.zeros_like(yrecv)
     zrecv[...] = jnp.zeros_like(zrecv)
     xyrecv[...] = jnp.zeros_like(xyrecv)
@@ -108,7 +109,6 @@
         z_others.append((me[0], me[1], lax.rem(me[2] + k, sizes[2])))
     for target in xy_others + z_others:
         pl.semaphore_signal(barrier, inc=1, device_id=target, device_id_type=MESH)
-    pl.semaphore_wait(barrier, count + len(xy_others) + len(z_others))
 
     lane = lax.broadcasted_iota(jnp.int32, (8, NZ), 1)
 
@@ -153,21 +153,22 @@
         for group in range(GROUPS):
             values = {}
             for m in sorted(set(Y_MEMBERS[0] + Y_MEMBERS[1] + Z_MEMBERS[0] + Z_MEMBERS[1])):
-                values[m] = state[0, SLOT[m], x + 1, rows_of(group), :]
+                values[m] = state[0][SLOT[m], x + 1, rows_of(group), :]
             pack(0, x, group, values)
         return carry
 
     lax.fori_loop(0, NX, first_pack, 0)
-    state[0, 0, 1, pl.ds(ROW0, NY), :] = state[0, SLOT[9], 1, pl.ds(ROW0, NY), :]
+    state[0][0, 1, pl.ds(ROW0, NY), :] = state[0][SLOT[9], 1, pl.ds(ROW0, NY), :]
+    pl.semaphore_wait(barrier, count + len(xy_others) + len(z_others))
     loads[20].wait()
     loads[21].wait()
 
     def message(b, m):
         cells = pl.ds(ROW0, NY)
         if m == 1:
-            return state.at[b, pl.ds(0, 5), 1, cells, :], state.at[b, pl.ds(0, 5), NX + 1, cells, :]
+            return state[b].at[pl.ds(0, 5), 1, cells, :], state[b].at[pl.ds(0, 5), NX + 1, cells, :]
         if m == 2:
-            return state.at[b, pl.ds(8, 5), NX, cells, :], state.at[b, pl.ds(8, 5), 0, cells, :]
+            return state[b].at[pl.ds(8, 5), NX, cells, :], state[b].at[pl.ds(8, 5), 0, cells, :]
         if m in (3, 4):
             return ysend.at[b, m - 3], yrecv.at[b, m - 3]
         if m in (5, 6):
@@ -210,6 +211,7 @@
             def _():
                 copy_of(t, b, m, at).wait_recv()
 
+    def sent(t, b):
         for m in range(1, 19):
             at, inside = beside(LATTICE[m], -1)
 
@@ -218,18 +220,18 @@
                 copy_of(t, b, m, at).wait_send()
 
     def unpack(b):
-        state[b, SLOT[9], NX + 1, pl.ds(ROW0, NY), :] = state[b, 0, NX + 1, pl.ds(ROW0, NY), :]
+        state[b][SLOT[9], NX + 1, pl.ds(ROW0, NY), :] = state[b][0, NX + 1, pl.ds(ROW0, NY), :]
         for side in range(2):
             row = ROW0 + NY if side == 0 else ROW0 - 1
             for i, m in enumerate(Y_MEMBERS[side]):
                 for x in range(NX):
-                    state[b, SLOT[m], x + 1, pl.ds(row, 1), :] = yrecv[b, side, i, pl.ds(x, 1), :]
+                    state[b][SLOT[m], x + 1, pl.ds(row, 1), :] = yrecv[b, side, i, pl.ds(x, 1), :]
         for m in range(7, 11):
             vector = LATTICE[m]
             plane = NX + 1 if vector[0] > 0 else 0
             row = ROW0 + NY if vector[1] > 0 else ROW0 - 1
             source = 0 if vector[0] > 0 else 7
-            state[b, SLOT[m], plane, pl.ds(row, 1), :] = xyrecv[b, m - 7, pl.ds(source, 1), :]
+            state[b][SLOT[m], plane, pl.ds(row, 1), :] = xyrecv[b, m - 7, pl.ds(source, 1), :]
         for m in range(11, 15):
             vector = LATTICE[m]
             side = 0 if vector[2] > 0 else 1
@@ -254,7 +256,7 @@
         read = []
         for m in range(19):
             vector = LATTICE[m]
-            value = state[b, SLOT[m], x + 1 + vector[0], rows_of(group, vector[1]), :]
+            value = state[b][SLOT[m], x + 1 + vector[0], rows_of(group, vector[1]), :]
             if vector[2] != 0:
                 side = 0 if vector[2] > 0 else 1
                 place = Z_MEMBERS[side].index(m) * LANES + x + 1 + vector[0]
@@ -339,8 +341,12 @@
                 u = [vel[STEPS - 1 - t, k, x, rows, :] for k in range(3)]
                 outputs, pressure = collide(read, u, solid[x, rows, :] == 1)
                 for m in range(19):
-                    state[nb, SLOT[m], x + 1, rows_of(group), :] = outputs[m]
-                pack(nb, x, group, outputs)
+                    if t < STEPS - 1:
+                        state[nb][SLOT[m], x + 1, rows_of(group), :] = outputs[m]
+                    else:
+                        out_ref[m, x, rows, :] = outputs[m]
+                if t < STEPS - 1:
+                    pack(nb, x, group, outputs)
                 upper = pressure.astype(jnp.bfloat16).astype(jnp.float32)
                 both = jnp.concatenate([upper, pressure - upper], axis=0).astype(jnp.bfloat16)
                 high = (ids[x, rows, :] >> 4).astype(jnp.float32)
@@ -357,8 +363,14 @@
             )
             return inner
 
-        lax.fori_loop(0, NX, one_plane, 0)
-        state[nb, 0, 1, pl.ds(ROW0, NY), :] = state[nb, SLOT[9], 1, pl.ds(ROW0, NY), :]
+        def two_planes(pair, inner):
+            one_plane(2 * pair, inner)
+            return one_plane(2 * pair + 1, inner)
+
+        lax.fori_loop(0, NX // 2, two_planes, 0)
+        sent(t, b)
+        if t < STEPS - 1:
+            state[nb][0, 1, pl.ds(ROW0, NY), :] = state[nb][SLOT[9], 1, pl.ds(ROW0, NY), :]
 
         own = jnp.where(same_y, acc[...], 0.0)
         total = jnp.sum(own.reshape(8, 16, NZ), axis=1)
@@ -394,24 +406,11 @@
             total = total + slots[k]
         return total
 
-    stores = []
-    for m in range(19):
-        stores.append(
-            pltpu.make_async_copy(
-                state.at[STEPS % 2, SLOT[m], pl.ds(1, NX), pl.ds(ROW0, NY), :],
-                out_ref.at[m],
-                out_sem.at[m],
-            )
-        )
-    for store in stores:
-        store.start()
     sums[pl.ds(STEPS, 8 - STEPS), :] = jnp.zeros((8 - STEPS, NZ), jnp.float32)
     total = gather_sum(sums[...], wall_xy, me[0] * sizes[1] + me[1], xy_others, xy_sem)
     total = gather_sum(total, wall_z, me[2], z_others, z_sem)
     cells_all = NX * NY * NZ * sizes[0] * sizes[1] * sizes[2]
     wall_ref[...] = total[:STEPS] * ((cells_all / (2.0 * WALLS)) ** (-0.5))
-    for store in stores:
-        store.wait()
 
 
 def body(terminal_adjoint, saved_velocity, solid_mask, wall_ids):
@@ -420,13 +419,14 @@
     return pl.pallas_call(
         functools.partial(kernel, sizes),
         out_shape=(
-            jax.ShapeDtypeStruct((19, NX, NY, NZ), f32),
+            pltpu.VMEM((19, NX, NY, NZ), f32),
             jax.ShapeDtypeStruct((STEPS, WALLS), f32),
         ),
         in_specs=[pl.BlockSpec(memory_space=pltpu.HBM)] * 4,
-        out_specs=(pl.BlockSpec(memory_space=pl.ANY), pl.BlockSpec(memory_space=pltpu.VMEM)),
+        out_specs=(pl.BlockSpec(memory_space=pltpu.VMEM),) * 2,
         scratch_shapes=[
-            vmem((2, SLOTS, NX + 2, ROWS, NZ), f32),
+            vmem((SLOTS, NX + 2, ROWS, NZ), f32),
+            vmem((SLOTS, NX + 2, ROWS, NZ), f32),
             vmem((STEPS, 3, NX, NY, NZ), f32),
             vmem((NX, NY, NZ), jnp.int32),
             vmem((NX, NY, NZ), jnp.int32),
@@ -444,14 +444,13 @@
             vmem((sizes[0] * sizes[1], 8, NZ), f32),
             vmem((sizes[2], 8, NZ), f32),
             pltpu.SemaphoreType.DMA((22,)),
-            pltpu.SemaphoreType.DMA((19,)),
             pltpu.SemaphoreType.DMA((STEPS, 18)),
             pltpu.SemaphoreType.DMA((STEPS, 18)),
             pltpu.SemaphoreType.DMA((2, max(1, sizes[0] * sizes[1] - 1))),
             pltpu.SemaphoreType.DMA((2, max(1, sizes[2] - 1))),
         ],
         compiler_params=pltpu.CompilerParams(
-            collective_id=0, has_side_effects=True, vmem_limit_bytes=48 * 2**20
+            collective_id=0, has_side_effects=True, vmem_limit_bytes=58 * 2**20
         ),
         name="adjoint_steps",
     )(terminal_adjoint, saved_velocity, solid_mask, wall_ids)

time: 75.6 us -> 62 us (0.82)
  local copies, waits for them, and re-layouts: 9.8 us -> 2.86 us
  Pallas kernels: 64.9 us -> 58.4 us
    unnamed x8 -> x4, local copies, waits for them, and re-layouts: 9.8 us -> 2.86 us
    pallas_call x1, Pallas kernels: 64.9 us -> 58.4 us  [body(): pl.pallas_call(functools.partial(kernel, sizes), out_shape=(pltpu.VMEM((1...]
where the time goes in v2:
time: 62 us; the launch traced here: 61.9 us
  Pallas kernels  58.4 us (94%)
  local copies, waits for them, and re-layouts  2.86 us (5%)
  between operations  0.65 us (1%)
    pallas_call x1, Pallas kernels, body(): pl.pallas_call(functools.partial(kernel, sizes), out_shape=(pltpu.VMEM((1...  58.4 us
    unnamed x4, local copies, waits for them, and re-layouts  2.86 us

profile of v2, /device:TPU:1, one launch (start us, length us, event | category | flops | bytes accessed | tf_op | source)
XLA Modules:
  0.0 61.9 jit_solution(17384979794075189665)
XLA Ops:
  0.6 58.4 %adjoint_steps.1 = (f32[19,16,32,128]{3,2,1,0:T(8,128)S(1)}, f32[4,128]{1,0:T(4,128)}) custom-call(f32[19,16,32,128]{3,2,1,0:T(8,128)} %adj_ref.1, f32[4,3,16,32,128]{4,3,2,1,0:T(8,128)} %vel_ref.1, s32[16,32,128]{2,1,0:T(8,128)} %solid_ref.1, s32[16,32,128]{2,1,0:T(8,128)} %ids_ref.1), custom_call_target="tpu_custom_call" | custom-call | tf_op jit(solution)/shard_map/adjoint_steps/pallas_call | solution.py:419
  59.0 0.0 copy-start
  59.0 2.3 %copy.8 = f32[19,16,32,128]{3,2,1,0:T(8,128)} copy(f32[19,16,32,128]{3,2,1,0:T(8,128)S(1)} %get-tuple-element.2) | data formatting | bytes 9961472
  61.3 0.0 copy-done
  61.3 0.6 copy.9
Async XLA Ops:
  59.0 2.3 %copy-start = (f32[4,128]{1,0:T(4,128)S(1)}, f32[4,128]{1,0:T(4,128)}, u32[]{:S(2)}) copy-start(f32[4,128]{1,0:T(4,128)} %get-tuple-element.7) | copy-start | bytes 6148

commit v3 on v2

--- a/solution.py
+++ b/solution.py
@@ -44,12 +44,15 @@
 Y_MEMBERS = ((7, 3, 15, 17, 10), (8, 4, 16, 18, 9))
 Z_MEMBERS = ((5, 11, 14, 15, 18), (6, 12, 13, 16, 17))
 LANES = NX + 2
+PAIRS = NX // 2
+QUARTER = PAIRS // 2
+INNER_MESSAGES = (3, 4, 5, 6, 15, 16, 17, 18)
 MESH = pl.DeviceIdType.MESH
 
 
 def kernel(
     sizes, adj_ref, vel_ref, solid_ref, ids_ref, out_ref, wall_ref,
-    state0, state1, vel, solid, ids, ysend, yrecv, zsend, zrecv, xyrecv, xzrecv, yzrecv,
+    state0, state1, vel, solid, ids, ysend, yrecv, zsend, zrecv, zinner, xyrecv, xzrecv, yzrecv,
     lo_hot, hi_part, acc, sums, wall_xy, wall_z,
     in_sem, send_sem, recv_sem, xy_sem, z_sem,
 ):
@@ -77,6 +80,7 @@
         state[b][:, NX + 1] = zero_plane
     yrecv[...] = jnp.zeros_like(yrecv)
     zrecv[...] = jnp.zeros_like(zrecv)
+    zinner[...] = jnp.zeros_like(zinner)
     xyrecv[...] = jnp.zeros_like(xyrecv)
     xzrecv[...] = jnp.zeros_like(xzrecv)
     yzrecv[...] = jnp.zeros_like(yzrecv)
@@ -130,108 +134,114 @@
 
     lax.fori_loop(0, NX, hot_plane, 0)
 
-    def pack(b, x, group, values):
+    def pack(b, pair, high, group, values):
+        part = pair // QUARTER
+        x = NX - 1 - pair if high else pair
+        row = lax.rem(pair, QUARTER)
+        row = 2 * QUARTER - 1 - row if high else row
         for side in range(2):
             rows = pl.ds(8 * group, 8)
-            packed = zsend[b, side, rows, :]
+            packed = zsend[b, part, side, rows, :]
             for i, m in enumerate(Z_MEMBERS[side]):
                 place = i * LANES + x + 1
                 moved = pltpu.roll(values[m], place + side, 1)
                 packed = jnp.where(lane == place, moved, packed)
-            zsend[b, side, rows, :] = packed
+            zsend[b, part, side, rows, :] = packed
         if group == 0:
             for i, m in enumerate(Y_MEMBERS[0]):
-                ysend[b, 0, i, pl.ds(x, 1), :] = values[m][0:1, :]
+                ysend[b, part, 0, i, pl.ds(row, 1), :] = values[m][0:1, :]
         if group == GROUPS - 1:
             for i, m in enumerate(Y_MEMBERS[1]):
-                ysend[b, 1, i, pl.ds(x, 1), :] = values[m][7:8, :]
+                ysend[b, part, 1, i, pl.ds(row, 1), :] = values[m][7:8, :]
 
     for m in range(19):
         loads[m].wait()
 
-    def first_pack(x, carry):
-        for group in range(GROUPS):
-            values = {}
-            for m in sorted(set(Y_MEMBERS[0] + Y_MEMBERS[1] + Z_MEMBERS[0] + Z_MEMBERS[1])):
-                values[m] = state[0][SLOT[m], x + 1, rows_of(group), :]
-            pack(0, x, group, values)
+    def first_pack(pair, carry):
+        for high in range(2):
+            x = NX - 1 - pair if high else pair
+            for group in range(GROUPS):
+                values = {}
+                for m in sorted(set(Y_MEMBERS[0] + Y_MEMBERS[1] + Z_MEMBERS[0] + Z_MEMBERS[1])):
+                    values[m] = state[0][SLOT[m], x + 1, rows_of(group), :]
+                pack(0, pair, high, group, values)
         return carry
 
-    lax.fori_loop(0, NX, first_pack, 0)
+    lax.fori_loop(0, PAIRS, first_pack, 0)
     state[0][0, 1, pl.ds(ROW0, NY), :] = state[0][SLOT[9], 1, pl.ds(ROW0, NY), :]
     pl.semaphore_wait(barrier, count + len(xy_others) + len(z_others))
-    loads[20].wait()
-    loads[21].wait()
-
-    def message(b, m):
+
+    def message(b, part, m):
         cells = pl.ds(ROW0, NY)
         if m == 1:
             return state[b].at[pl.ds(0, 5), 1, cells, :], state[b].at[pl.ds(0, 5), NX + 1, cells, :]
         if m == 2:
             return state[b].at[pl.ds(8, 5), NX, cells, :], state[b].at[pl.ds(8, 5), 0, cells, :]
         if m in (3, 4):
-            return ysend.at[b, m - 3], yrecv.at[b, m - 3]
+            return ysend.at[b, part, m - 3], yrecv.at[b, part, m - 3]
         if m in (5, 6):
-            return zsend.at[b, m - 5], zrecv.at[b, m - 5, cells, :]
+            landing = zinner if part else zrecv
+            return zsend.at[b, part, m - 5], landing.at[b, m - 5, cells, :]
         vector = LATTICE[m]
         if m <= 10:
             side = 0 if vector[1] > 0 else 1
-            start = 0 if vector[0] > 0 else NX - 8
-            member = Y_MEMBERS[side].index(m)
-            return ysend.at[b, side, member, pl.ds(start, 8), :], xyrecv.at[b, m - 7]
+            return ysend.at[b, 0, side, Y_MEMBERS[side].index(m)], xyrecv.at[b, m - 7]
         side = 0 if vector[2] > 0 else 1
         if m <= 14:
-            return zsend.at[b, side], xzrecv.at[b, m - 11]
+            return zsend.at[b, 0, side], xzrecv.at[b, m - 11]
         start = 0 if vector[1] > 0 else NY - 8
-        return zsend.at[b, side, pl.ds(start, 8), :], yzrecv.at[b, m - 15]
-
-    def copy_of(t, b, m, target):
-        source, landing = message(b, m)
-        return pltpu.make_async_remote_copy(
-            src_ref=source,
-            dst_ref=landing,
-            send_sem=send_sem.at[t, m - 1],
-            recv_sem=recv_sem.at[t, m - 1],
-            device_id=target,
-            device_id_type=MESH,
-        )
-
-    def exchange(t, b):
-        for m in range(1, 19):
-            at, inside = beside(LATTICE[m], -1)
+        return zsend.at[b, part, side, pl.ds(start, 8), :], yzrecv.at[b, part, m - 15]
+
+    def copies_of(t, part, sign, act):
+        for m in INNER_MESSAGES if part else range(1, 19):
+            at, inside = beside(LATTICE[m], sign)
+            source, landing = message(t % 2, part, m)
+            copy = pltpu.make_async_remote_copy(
+                src_ref=source,
+                dst_ref=landing,
+                send_sem=send_sem.at[t, part, m - 1],
+                recv_sem=recv_sem.at[t, part, m - 1],
+                device_id=at,
+                device_id_type=MESH,
+            )
 
             @pl.when(inside)
             def _():
-                copy_of(t, b, m, at).start()
-
-        for m in range(1, 19):
-            at, inside = beside(LATTICE[m], 1)
-
-            @pl.when(inside)
-            def _():
-                copy_of(t, b, m, at).wait_recv()
-
-    def sent(t, b):
-        for m in range(1, 19):
-            at, inside = beside(LATTICE[m], -1)
-
-            @pl.when(inside)
-            def _():
-                copy_of(t, b, m, at).wait_send()
-
-    def unpack(b):
-        state[b][SLOT[9], NX + 1, pl.ds(ROW0, NY), :] = state[b][0, NX + 1, pl.ds(ROW0, NY), :]
+                act(copy)
+
+    def send(t, part):
+        copies_of(t, part, -1, lambda copy: copy.start())
+
+    def sent(t, part):
+        copies_of(t, part, -1, lambda copy: copy.wait_send())
+
+    def receive(t, part):
+        copies_of(t, part, 1, lambda copy: copy.wait_recv())
+
+    def unpack_rows(b, part):
         for side in range(2):
             row = ROW0 + NY if side == 0 else ROW0 - 1
             for i, m in enumerate(Y_MEMBERS[side]):
-                for x in range(NX):
-                    state[b][SLOT[m], x + 1, pl.ds(row, 1), :] = yrecv[b, side, i, pl.ds(x, 1), :]
+                for k in range(2 * QUARTER):
+                    x = QUARTER + k if part else k if k < QUARTER else NX - 2 * QUARTER + k
+                    state[b][SLOT[m], x + 1, pl.ds(row, 1), :] = yrecv[b, part, side, i, pl.ds(k, 1), :]
+        for m in range(15, 19):
+            vector = LATTICE[m]
+            side = 0 if vector[2] > 0 else 1
+            row = ROW0 + NY if vector[1] > 0 else ROW0 - 1
+            source = 0 if vector[1] > 0 else 7
+            landing = zinner if part else zrecv
+            landing[b, side, pl.ds(row, 1), :] = yzrecv[b, part, m - 15, pl.ds(source, 1), :]
+
+    def unpack_outer(b):
+        state[b][SLOT[9], NX + 1, pl.ds(ROW0, NY), :] = state[b][0, NX + 1, pl.ds(ROW0, NY), :]
+        unpack_rows(b, 0)
         for m in range(7, 11):
             vector = LATTICE[m]
-            plane = NX + 1 if vector[0] > 0 else 0
+            plane_at = NX + 1 if vector[0] > 0 else 0
             row = ROW0 + NY if vector[1] > 0 else ROW0 - 1
             source = 0 if vector[0] > 0 else 7
-            state[b][SLOT[m], plane, pl.ds(row, 1), :] = xyrecv[b, m - 7, pl.ds(source, 1), :]
+            state[b][SLOT[m], plane_at, pl.ds(row, 1), :] = xyrecv[b, m - 7, pl.ds(source, 1), :]
         for m in range(11, 15):
             vector = LATTICE[m]
             side = 0 if vector[2] > 0 else 1
@@ -245,12 +255,23 @@
                 zrecv[b, side, rows_of(group), :] = jnp.where(
                     lane == place, moved, zrecv[b, side, rows_of(group), :]
                 )
-        for m in range(15, 19):
-            vector = LATTICE[m]
-            side = 0 if vector[2] > 0 else 1
-            row = ROW0 + NY if vector[1] > 0 else ROW0 - 1
-            source = 0 if vector[1] > 0 else 7
-            zrecv[b, side, pl.ds(row, 1), :] = yzrecv[b, m - 15, pl.ds(source, 1), :]
+
+    in_plane = lax.rem(lane, LANES)
+    inner_lane = (in_plane > QUARTER) & (in_plane <= NX - QUARTER)
+
+    def unpack_inner(b):
+        unpack_rows(b, 1)
+        for side in range(2):
+            for k in range(ROWS // 8):
+                rows = pl.ds(8 * k, 8)
+                zrecv[b, side, rows, :] = jnp.where(
+                    inner_lane, zinner[b, side, rows, :], zrecv[b, side, rows, :]
+                )
+
+    send(0, 0)
+    send(0, 1)
+    loads[20].wait()
+    loads[21].wait()
 
     def pull(b, x, group):
         read = []
@@ -330,47 +351,62 @@
     def one_step(t):
         b = t % 2
         nb = 1 - b
-        exchange(t, b)
-        unpack(b)
+        last = t == STEPS - 1
         acc[...] = jnp.zeros_like(acc)
-
-        def one_plane(x, inner):
+        receive(t, 0)
+        unpack_outer(b)
+
+        def one_plane(pair, high):
+            x = NX - 1 - pair if high else pair
             for group in range(GROUPS):
                 rows = pl.ds(8 * group, 8)
                 read = pull(b, x, group)
                 u = [vel[STEPS - 1 - t, k, x, rows, :] for k in range(3)]
                 outputs, pressure = collide(read, u, solid[x, rows, :] == 1)
                 for m in range(19):
-                    if t < STEPS - 1:
+                    if last:
+                        out_ref[m, x, rows, :] = outputs[m]
+                    else:
                         state[nb][SLOT[m], x + 1, rows_of(group), :] = outputs[m]
-                    else:
-                        out_ref[m, x, rows, :] = outputs[m]
-                if t < STEPS - 1:
-                    pack(nb, x, group, outputs)
+                if not last:
+                    pack(nb, pair, high, group, outputs)
                 upper = pressure.astype(jnp.bfloat16).astype(jnp.float32)
                 both = jnp.concatenate([upper, pressure - upper], axis=0).astype(jnp.bfloat16)
-                high = (ids[x, rows, :] >> 4).astype(jnp.float32)
-                high = jnp.concatenate([high, high], axis=0).astype(jnp.bfloat16)
+                bits = (ids[x, rows, :] >> 4).astype(jnp.float32)
+                bits = jnp.concatenate([bits, bits], axis=0).astype(jnp.bfloat16)
                 for h in range(8):
-                    hi_part[pl.ds(16 * h, 16), pl.ds(NZ * group, NZ)] = jnp.where(
-                        high == h, both, jnp.zeros_like(both)
+                    hi_part[high, pl.ds(16 * h, 16), pl.ds(NZ * group, NZ)] = jnp.where(
+                        bits == h, both, jnp.zeros_like(both)
                     )
             acc[...] += lax.dot_general(
-                hi_part[...],
+                hi_part[high],
                 lo_hot[x],
                 (((1,), (1,)), ((), ())),
                 preferred_element_type=jnp.float32,
             )
-            return inner
-
-        def two_planes(pair, inner):
-            one_plane(2 * pair, inner)
-            return one_plane(2 * pair + 1, inner)
-
-        lax.fori_loop(0, NX // 2, two_planes, 0)
-        sent(t, b)
-        if t < STEPS - 1:
-            state[nb][0, 1, pl.ds(ROW0, NY), :] = state[nb][SLOT[9], 1, pl.ds(ROW0, NY), :]
+
+        def one_pair(pair, carry):
+            @pl.when(pair == QUARTER - 1)
+            def _():
+                receive(t, 1)
+                unpack_inner(b)
+
+            if not last:
+
+                @pl.when(pair == QUARTER)
+                def _():
+                    state[nb][0, 1, pl.ds(ROW0, NY), :] = state[nb][SLOT[9], 1, pl.ds(ROW0, NY), :]
+                    send(t + 1, 0)
+
+            one_plane(pair, 0)
+            one_plane(pair, 1)
+            return carry
+
+        lax.fori_loop(0, PAIRS, one_pair, 0)
+        if not last:
+            send(t + 1, 1)
+        sent(t, 0)
+        sent(t, 1)
 
         own = jnp.where(same_y, acc[...], 0.0)
         total = jnp.sum(own.reshape(8, 16, NZ), axis=1)
@@ -430,22 +466,23 @@
             vmem((STEPS, 3, NX, NY, NZ), f32),
             vmem((NX, NY, NZ), jnp.int32),
             vmem((NX, NY, NZ), jnp.int32),
-            vmem((2, 2, 5, NX, NZ), f32),
-            vmem((2, 2, 5, NX, NZ), f32),
-            vmem((2, 2, NY, NZ), f32),
+            vmem((2, 2, 2, 5, 2 * QUARTER, NZ), f32),
+            vmem((2, 2, 2, 5, 2 * QUARTER, NZ), f32),
+            vmem((2, 2, 2, NY, NZ), f32),
+            vmem((2, 2, ROWS, NZ), f32),
             vmem((2, 2, ROWS, NZ), f32),
             vmem((2, 4, 8, NZ), f32),
             vmem((2, 4, NY, NZ), f32),
-            vmem((2, 4, 8, NZ), f32),
+            vmem((2, 2, 4, 8, NZ), f32),
             vmem((NX, 128, GROUPS * NZ), jnp.bfloat16),
-            vmem((128, GROUPS * NZ), jnp.bfloat16),
+            vmem((2, 128, GROUPS * NZ), jnp.bfloat16),
             vmem((128, NZ), f32),
             vmem((8, NZ), f32),
             vmem((sizes[0] * sizes[1], 8, NZ), f32),
             vmem((sizes[2], 8, NZ), f32),
             pltpu.SemaphoreType.DMA((22,)),
-            pltpu.SemaphoreType.DMA((STEPS, 18)),
-            pltpu.SemaphoreType.DMA((STEPS, 18)),
+            pltpu.SemaphoreType.DMA((STEPS, 2, 18)),
+            pltpu.SemaphoreType.DMA((STEPS, 2, 18)),
             pltpu.SemaphoreType.DMA((2, max(1, sizes[0] * sizes[1] - 1))),
             pltpu.SemaphoreType.DMA((2, max(1, sizes[2] - 1))),
         ],

time: 62 us -> 58.3 us (0.940)
  Pallas kernels: 58.4 us -> 54.7 us
    pallas_call x1, Pallas kernels: 58.4 us -> 54.7 us  [body(): pl.pallas_call(functools.partial(kernel, sizes), out_shape=(pltpu.VMEM((1...]
where the time goes in v3:
time: 58.3 us; the launch traced here: 58.2 us
  Pallas kernels  54.7 us (94%)
  local copies, waits for them, and re-layouts  2.86 us (5%)
  between operations  0.65 us (1%)
    pallas_call x1, Pallas kernels, body(): pl.pallas_call(functools.partial(kernel, sizes), out_shape=(pltpu.VMEM((1...  54.7 us
    unnamed x4, local copies, waits for them, and re-layouts  2.86 us

profile of v3, /device:TPU:1, one launch (start us, length us, event | category | flops | bytes accessed | tf_op | source)
XLA Modules:
  0.0 58.2 jit_solution(1116615560570380368)
XLA Ops:
  0.6 54.7 %adjoint_steps.1 = (f32[19,16,32,128]{3,2,1,0:T(8,128)S(1)}, f32[4,128]{1,0:T(4,128)}) custom-call(f32[19,16,32,128]{3,2,1,0:T(8,128)} %adj_ref.1, f32[4,3,16,32,128]{4,3,2,1,0:T(8,128)} %vel_ref.1, s32[16,32,128]{2,1,0:T(8,128)} %solid_ref.1, s32[16,32,128]{2,1,0:T(8,128)} %ids_ref.1), custom_call_target="tpu_custom_call" | custom-call | tf_op jit(solution)/shard_map/adjoint_steps/pallas_call | solution.py:455
  55.3 0.0 copy-start
  55.3 2.3 %copy.8 = f32[19,16,32,128]{3,2,1,0:T(8,128)} copy(f32[19,16,32,128]{3,2,1,0:T(8,128)S(1)} %get-tuple-element.2) | data formatting | bytes 9961472
  57.6 0.0 copy-done
  57.6 0.6 copy.9
Async XLA Ops:
  55.3 2.3 %copy-start = (f32[4,128]{1,0:T(4,128)S(1)}, f32[4,128]{1,0:T(4,128)}, u32[]{:S(2)}) copy-start(f32[4,128]{1,0:T(4,128)} %get-tuple-element.7) | copy-start | bytes 6148

commit v4 on v3

--- a/solution.py
+++ b/solution.py
@@ -45,7 +45,8 @@
 Z_MEMBERS = ((5, 11, 14, 15, 18), (6, 12, 13, 16, 17))
 LANES = NX + 2
 PAIRS = NX // 2
-QUARTER = PAIRS // 2
+PARTS = 2
+SPAN = PAIRS // PARTS
 INNER_MESSAGES = (3, 4, 5, 6, 15, 16, 17, 18)
 MESH = pl.DeviceIdType.MESH
 
@@ -74,10 +75,10 @@
     for load in loads:
         load.start()
 
-    zero_plane = jnp.zeros((SLOTS, ROWS, NZ), jnp.float32)
     for b in range(2):
-        state[b][:, 0] = zero_plane
-        state[b][:, NX + 1] = zero_plane
+        state[b][8:13, 0] = jnp.zeros((5, ROWS, NZ), jnp.float32)
+        state[b][0:5, NX + 1] = jnp.zeros((5, ROWS, NZ), jnp.float32)
+        state[b][SLOT[9], NX + 1] = jnp.zeros((ROWS, NZ), jnp.float32)
     yrecv[...] = jnp.zeros_like(yrecv)
     zrecv[...] = jnp.zeros_like(zrecv)
     zinner[...] = jnp.zeros_like(zinner)
@@ -119,7 +120,6 @@
     def rows_of(group, shift=0):
         return pl.ds(ROW0 + 8 * group + shift, 8)
 
-    loads[19].wait()
     low_iota = lax.broadcasted_iota(jnp.int32, (16, NZ), 0)
 
     def hot_plane(x, carry):
@@ -132,13 +132,12 @@
                 ).astype(jnp.bfloat16)
         return carry
 
-    lax.fori_loop(0, NX, hot_plane, 0)
 
     def pack(b, pair, high, group, values):
-        part = pair // QUARTER
+        part = pair // SPAN
         x = NX - 1 - pair if high else pair
-        row = lax.rem(pair, QUARTER)
-        row = 2 * QUARTER - 1 - row if high else row
+        row = lax.rem(pair, SPAN)
+        row = 7 - row if high else row
         for side in range(2):
             rows = pl.ds(8 * group, 8)
             packed = zsend[b, part, side, rows, :]
@@ -154,8 +153,6 @@
             for i, m in enumerate(Y_MEMBERS[1]):
                 ysend[b, part, 1, i, pl.ds(row, 1), :] = values[m][7:8, :]
 
-    for m in range(19):
-        loads[m].wait()
 
     def first_pack(pair, carry):
         for high in range(2):
@@ -167,9 +164,6 @@
                 pack(0, pair, high, group, values)
         return carry
 
-    lax.fori_loop(0, PAIRS, first_pack, 0)
-    state[0][0, 1, pl.ds(ROW0, NY), :] = state[0][SLOT[9], 1, pl.ds(ROW0, NY), :]
-    pl.semaphore_wait(barrier, count + len(xy_others) + len(z_others))
 
     def message(b, part, m):
         cells = pl.ds(ROW0, NY)
@@ -180,7 +174,7 @@
         if m in (3, 4):
             return ysend.at[b, part, m - 3], yrecv.at[b, part, m - 3]
         if m in (5, 6):
-            landing = zinner if part else zrecv
+            landing = zinner.at[part - 1] if part else zrecv
             return zsend.at[b, part, m - 5], landing.at[b, m - 5, cells, :]
         vector = LATTICE[m]
         if m <= 10:
@@ -222,15 +216,18 @@
         for side in range(2):
             row = ROW0 + NY if side == 0 else ROW0 - 1
             for i, m in enumerate(Y_MEMBERS[side]):
-                for k in range(2 * QUARTER):
-                    x = QUARTER + k if part else k if k < QUARTER else NX - 2 * QUARTER + k
-                    state[b][SLOT[m], x + 1, pl.ds(row, 1), :] = yrecv[b, part, side, i, pl.ds(k, 1), :]
+                for k in range(SPAN):
+                    pair = part * SPAN + k
+                    for x, source in ((pair, k), (NX - 1 - pair, 7 - k)):
+                        state[b][SLOT[m], x + 1, pl.ds(row, 1), :] = yrecv[
+                            b, part, side, i, pl.ds(source, 1), :
+                        ]
         for m in range(15, 19):
             vector = LATTICE[m]
             side = 0 if vector[2] > 0 else 1
             row = ROW0 + NY if vector[1] > 0 else ROW0 - 1
             source = 0 if vector[1] > 0 else 7
-            landing = zinner if part else zrecv
+            landing = zinner.at[part - 1] if part else zrecv
             landing[b, side, pl.ds(row, 1), :] = yzrecv[b, part, m - 15, pl.ds(source, 1), :]
 
     def unpack_outer(b):
@@ -257,19 +254,27 @@
                 )
 
     in_plane = lax.rem(lane, LANES)
-    inner_lane = (in_plane > QUARTER) & (in_plane <= NX - QUARTER)
-
-    def unpack_inner(b):
-        unpack_rows(b, 1)
+
+    def unpack_inner(b, part):
+        inner_lane = (in_plane > part * SPAN) & (in_plane <= NX - part * SPAN)
+        unpack_rows(b, part)
         for side in range(2):
             for k in range(ROWS // 8):
                 rows = pl.ds(8 * k, 8)
                 zrecv[b, side, rows, :] = jnp.where(
-                    inner_lane, zinner[b, side, rows, :], zrecv[b, side, rows, :]
+                    inner_lane, zinner[part - 1, b, side, rows, :], zrecv[b, side, rows, :]
                 )
 
-    send(0, 0)
-    send(0, 1)
+    for m in range(19):
+        loads[m].wait()
+    pl.semaphore_wait(barrier, count + len(xy_others) + len(z_others))
+    for part in range(PARTS):
+        lax.fori_loop(part * SPAN, (part + 1) * SPAN, first_pack, 0)
+        if part == 0:
+            state[0][0, 1, pl.ds(ROW0, NY), :] = state[0][SLOT[9], 1, pl.ds(ROW0, NY), :]
+        send(0, part)
+    loads[19].wait()
+    lax.fori_loop(0, NX, hot_plane, 0)
     loads[20].wait()
     loads[21].wait()
 
@@ -386,17 +391,21 @@
             )
 
         def one_pair(pair, carry):
-            @pl.when(pair == QUARTER - 1)
-            def _():
-                receive(t, 1)
-                unpack_inner(b)
-
-            if not last:
-
-                @pl.when(pair == QUARTER)
+            for part in range(1, PARTS):
+
+                @pl.when(pair == part * SPAN - 1)
                 def _():
-                    state[nb][0, 1, pl.ds(ROW0, NY), :] = state[nb][SLOT[9], 1, pl.ds(ROW0, NY), :]
-                    send(t + 1, 0)
+                    receive(t, part)
+                    unpack_inner(b, part)
+
+                if not last:
+
+                    @pl.when(pair == part * SPAN)
+                    def _():
+                        if part == 1:
+                            cells = pl.ds(ROW0, NY)
+                            state[nb][0, 1, cells, :] = state[nb][SLOT[9], 1, cells, :]
+                        send(t + 1, part - 1)
 
             one_plane(pair, 0)
             one_plane(pair, 1)
@@ -404,9 +413,9 @@
 
         lax.fori_loop(0, PAIRS, one_pair, 0)
         if not last:
-            send(t + 1, 1)
-        sent(t, 0)
-        sent(t, 1)
+            send(t + 1, PARTS - 1)
+        for part in range(PARTS):
+            sent(t, part)
 
         own = jnp.where(same_y, acc[...], 0.0)
         total = jnp.sum(own.reshape(8, 16, NZ), axis=1)
@@ -466,14 +475,14 @@
             vmem((STEPS, 3, NX, NY, NZ), f32),
             vmem((NX, NY, NZ), jnp.int32),
             vmem((NX, NY, NZ), jnp.int32),
-            vmem((2, 2, 2, 5, 2 * QUARTER, NZ), f32),
-            vmem((2, 2, 2, 5, 2 * QUARTER, NZ), f32),
-            vmem((2, 2, 2, NY, NZ), f32),
+            vmem((2, PARTS, 2, 5, 8, NZ), f32),
+            vmem((2, PARTS, 2, 5, 8, NZ), f32),
+            vmem((2, PARTS, 2, NY, NZ), f32),
             vmem((2, 2, ROWS, NZ), f32),
-            vmem((2, 2, ROWS, NZ), f32),
+            vmem((PARTS - 1, 2, 2, ROWS, NZ), f32),
             vmem((2, 4, 8, NZ), f32),
             vmem((2, 4, NY, NZ), f32),
-            vmem((2, 2, 4, 8, NZ), f32),
+            vmem((2, PARTS, 4, 8, NZ), f32),
             vmem((NX, 128, GROUPS * NZ), jnp.bfloat16),
             vmem((2, 128, GROUPS * NZ), jnp.bfloat16),
             vmem((128, NZ), f32),
@@ -481,8 +490,8 @@
             vmem((sizes[0] * sizes[1], 8, NZ), f32),
             vmem((sizes[2], 8, NZ), f32),
             pltpu.SemaphoreType.DMA((22,)),
-            pltpu.SemaphoreType.DMA((STEPS, 2, 18)),
-            pltpu.SemaphoreType.DMA((STEPS, 2, 18)),
+            pltpu.SemaphoreType.DMA((STEPS, PARTS, 18)),
+            pltpu.SemaphoreType.DMA((STEPS, PARTS, 18)),
             pltpu.SemaphoreType.DMA((2, max(1, sizes[0] * sizes[1] - 1))),
             pltpu.SemaphoreType.DMA((2, max(1, sizes[2] - 1))),
         ],

time: 58.3 us -> 56.8 us (0.974)
  Pallas kernels: 54.7 us -> 53.2 us
    pallas_call x1, Pallas kernels: 54.7 us -> 53.2 us  [body(): pl.pallas_call(functools.partial(kernel, sizes), out_shape=(pltpu.VMEM((1...]
where the time goes in v4:
time: 56.8 us; the launch traced here: 56.7 us
  Pallas kernels  53.2 us (94%)
  local copies, waits for them, and re-layouts  2.86 us (5%)
  between operations  0.65 us (1%)
    pallas_call x1, Pallas kernels, body(): pl.pallas_call(functools.partial(kernel, sizes), out_shape=(pltpu.VMEM((1...  53.2 us
    unnamed x4, local copies, waits for them, and re-layouts  2.86 us

profile of v4, /device:TPU:1, one launch (start us, length us, event | category | flops | bytes accessed | tf_op | source)
XLA Modules:
  0.0 56.7 jit_solution(7017124600988740761)
XLA Ops:
  0.6 53.2 %adjoint_steps.1 = (f32[19,16,32,128]{3,2,1,0:T(8,128)S(1)}, f32[4,128]{1,0:T(4,128)}) custom-call(f32[19,16,32,128]{3,2,1,0:T(8,128)} %adj_ref.1, f32[4,3,16,32,128]{4,3,2,1,0:T(8,128)} %vel_ref.1, s32[16,32,128]{2,1,0:T(8,128)} %solid_ref.1, s32[16,32,128]{2,1,0:T(8,128)} %ids_ref.1), custom_call_target="tpu_custom_call" | custom-call | tf_op jit(solution)/shard_map/adjoint_steps/pallas_call | solution.py:464
  53.8 0.0 copy-start
  53.8 2.3 %copy.8 = f32[19,16,32,128]{3,2,1,0:T(8,128)} copy(f32[19,16,32,128]{3,2,1,0:T(8,128)S(1)} %get-tuple-element.2) | data formatting | bytes 9961472
  56.1 0.0 copy-done
  56.1 0.6 %copy.9 = f32[4,128]{1,0:T(4,128)} copy(f32[4,128]{1,0:T(4,128)S(1)} %copy-done) | data formatting | bytes 4096
Async XLA Ops:
  53.8 2.3 %copy-start = (f32[4,128]{1,0:T(4,128)S(1)}, f32[4,128]{1,0:T(4,128)}, u32[]{:S(2)}) copy-start(f32[4,128]{1,0:T(4,128)} %get-tuple-element.7) | copy-start | bytes 6148

commit v5 on v4

--- a/solution.py
+++ b/solution.py
@@ -47,7 +47,9 @@
 PAIRS = NX // 2
 PARTS = 2
 SPAN = PAIRS // PARTS
-INNER_MESSAGES = (3, 4, 5, 6, 15, 16, 17, 18)
+ACROSS = PARTS
+ALONG_MESSAGES = (3, 4, 5, 6, 15, 16, 17, 18)
+ACROSS_MESSAGES = (1, 2, 7, 8, 9, 10, 11, 12, 13, 14)
 MESH = pl.DeviceIdType.MESH
 
 
@@ -187,7 +189,7 @@
         return zsend.at[b, part, side, pl.ds(start, 8), :], yzrecv.at[b, part, m - 15]
 
     def copies_of(t, part, sign, act):
-        for m in INNER_MESSAGES if part else range(1, 19):
+        for m in ACROSS_MESSAGES if part == ACROSS else ALONG_MESSAGES:
             at, inside = beside(LATTICE[m], sign)
             source, landing = message(t % 2, part, m)
             copy = pltpu.make_async_remote_copy(
@@ -230,9 +232,8 @@
             landing = zinner.at[part - 1] if part else zrecv
             landing[b, side, pl.ds(row, 1), :] = yzrecv[b, part, m - 15, pl.ds(source, 1), :]
 
-    def unpack_outer(b):
+    def unpack_across(b):
         state[b][SLOT[9], NX + 1, pl.ds(ROW0, NY), :] = state[b][0, NX + 1, pl.ds(ROW0, NY), :]
-        unpack_rows(b, 0)
         for m in range(7, 11):
             vector = LATTICE[m]
             plane_at = NX + 1 if vector[0] > 0 else 0
@@ -273,6 +274,8 @@
         if part == 0:
             state[0][0, 1, pl.ds(ROW0, NY), :] = state[0][SLOT[9], 1, pl.ds(ROW0, NY), :]
         send(0, part)
+        if part == 0:
+            send(0, ACROSS)
     loads[19].wait()
     lax.fori_loop(0, NX, hot_plane, 0)
     loads[20].wait()
@@ -359,7 +362,7 @@
         last = t == STEPS - 1
         acc[...] = jnp.zeros_like(acc)
         receive(t, 0)
-        unpack_outer(b)
+        unpack_rows(b, 0)
 
         def one_plane(pair, high):
             x = NX - 1 - pair if high else pair
@@ -390,22 +393,32 @@
                 preferred_element_type=jnp.float32,
             )
 
-        def one_pair(pair, carry):
+        def one_pair(i, carry):
+            later = lax.div(i + PAIRS - 3, PAIRS)
+            pair = later * i + (1 - later) * lax.rem(i + 1, 3)
+
+            @pl.when(i == 2)
+            def _():
+                receive(t, ACROSS)
+                unpack_across(b)
+
             for part in range(1, PARTS):
 
-                @pl.when(pair == part * SPAN - 1)
+                @pl.when(i == part * SPAN - 1)
                 def _():
                     receive(t, part)
                     unpack_inner(b, part)
 
                 if not last:
 
-                    @pl.when(pair == part * SPAN)
+                    @pl.when(i == part * SPAN)
                     def _():
                         if part == 1:
                             cells = pl.ds(ROW0, NY)
                             state[nb][0, 1, cells, :] = state[nb][SLOT[9], 1, cells, :]
                         send(t + 1, part - 1)
+                        if part == 1:
+                            send(t + 1, ACROSS)
 
             one_plane(pair, 0)
             one_plane(pair, 1)
@@ -414,7 +427,7 @@
         lax.fori_loop(0, PAIRS, one_pair, 0)
         if not last:
             send(t + 1, PARTS - 1)
-        for part in range(PARTS):
+        for part in range(PARTS + 1):
             sent(t, part)
 
         own = jnp.where(same_y, acc[...], 0.0)
@@ -490,8 +503,8 @@
             vmem((sizes[0] * sizes[1], 8, NZ), f32),
             vmem((sizes[2], 8, NZ), f32),
             pltpu.SemaphoreType.DMA((22,)),
-            pltpu.SemaphoreType.DMA((STEPS, PARTS, 18)),
-            pltpu.SemaphoreType.DMA((STEPS, PARTS, 18)),
+            pltpu.SemaphoreType.DMA((STEPS, PARTS + 1, 18)),
+            pltpu.SemaphoreType.DMA((STEPS, PARTS + 1, 18)),
             pltpu.SemaphoreType.DMA((2, max(1, sizes[0] * sizes[1] - 1))),
             pltpu.SemaphoreType.DMA((2, max(1, sizes[2] - 1))),
         ],

time: 56.8 us -> 55.7 us (0.981)
  Pallas kernels: 53.2 us -> 52.1 us
    pallas_call x1, Pallas kernels: 53.2 us -> 52.1 us  [body(): pl.pallas_call(functools.partial(kernel, sizes), out_shape=(pltpu.VMEM((1...]
where the time goes in v5:
time: 55.7 us; the launch traced here: 55.6 us
  Pallas kernels  52.1 us (94%)
  local copies, waits for them, and re-layouts  2.86 us (5%)
  between operations  0.65 us (1%)
    pallas_call x1, Pallas kernels, body(): pl.pallas_call(functools.partial(kernel, sizes), out_shape=(pltpu.VMEM((1...  52.1 us
    unnamed x4, local copies, waits for them, and re-layouts  2.86 us

profile of v5, /device:TPU:1, one launch (start us, length us, event | category | flops | bytes accessed | tf_op | source)
XLA Modules:
  0.0 55.6 jit_solution(14067256441977414982)
XLA Ops:
  0.6 52.1 %adjoint_steps.1 = (f32[19,16,32,128]{3,2,1,0:T(8,128)S(1)}, f32[4,128]{1,0:T(4,128)}) custom-call(f32[19,16,32,128]{3,2,1,0:T(8,128)} %adj_ref.1, f32[4,3,16,32,128]{4,3,2,1,0:T(8,128)} %vel_ref.1, s32[16,32,128]{2,1,0:T(8,128)} %solid_ref.1, s32[16,32,128]{2,1,0:T(8,128)} %ids_ref.1), custom_call_target="tpu_custom_call" | custom-call | tf_op jit(solution)/shard_map/adjoint_steps/pallas_call | solution.py:477
  52.7 0.0 copy-start
  52.7 2.3 %copy.8 = f32[19,16,32,128]{3,2,1,0:T(8,128)} copy(f32[19,16,32,128]{3,2,1,0:T(8,128)S(1)} %get-tuple-element.2) | data formatting | bytes 9961472
  55.0 0.0 copy-done
  55.0 0.6 %copy.9 = f32[4,128]{1,0:T(4,128)} copy(f32[4,128]{1,0:T(4,128)S(1)} %copy-done) | data formatting | bytes 4096
Async XLA Ops:
  52.7 2.3 %copy-start = (f32[4,128]{1,0:T(4,128)S(1)}, f32[4,128]{1,0:T(4,128)}, u32[]{:S(2)}) copy-start(f32[4,128]{1,0:T(4,128)} %get-tuple-element.7) | copy-start | bytes 6148

commit v6 on v5

--- a/solution.py
+++ b/solution.py
@@ -478,7 +478,7 @@
         functools.partial(kernel, sizes),
         out_shape=(
             pltpu.VMEM((19, NX, NY, NZ), f32),
-            jax.ShapeDtypeStruct((STEPS, WALLS), f32),
+            pltpu.VMEM((STEPS, WALLS), f32),
         ),
         in_specs=[pl.BlockSpec(memory_space=pltpu.HBM)] * 4,
         out_specs=(pl.BlockSpec(memory_space=pltpu.VMEM),) * 2,

time: 55.7 us -> 55.1 us (0.989)
  Pallas kernels: 52.1 us -> 51.5 us
    pallas_call x1, Pallas kernels: 52.1 us -> 51.5 us  [body(): pl.pallas_call(functools.partial(kernel, sizes), out_shape=(pltpu.VMEM((1...]
    unnamed x4 -> x2, local copies, waits for them, and re-layouts: 2.86 us -> 2.85 us
where the time goes in v6:
time: 55.1 us; the launch traced here: 54.9 us
  Pallas kernels  51.5 us (93%)
  local copies, waits for them, and re-layouts  2.85 us (5%)
  between operations  0.64 us (1%)
    pallas_call x1, Pallas kernels, body(): pl.pallas_call(functools.partial(kernel, sizes), out_shape=(pltpu.VMEM((1...  51.5 us
    unnamed x2, local copies, waits for them, and re-layouts  2.85 us

profile of v6, /device:TPU:1, one launch (start us, length us, event | category | flops | bytes accessed | tf_op | source)
XLA Modules:
  0.0 54.9 jit_solution(4207094629698783973)
XLA Ops:
  0.6 51.5 %adjoint_steps.1 = (f32[19,16,32,128]{3,2,1,0:T(8,128)S(1)}, f32[4,128]{1,0:T(4,128)S(1)}) custom-call(f32[19,16,32,128]{3,2,1,0:T(8,128)} %adj_ref.1, f32[4,3,16,32,128]{4,3,2,1,0:T(8,128)} %vel_ref.1, s32[16,32,128]{2,1,0:T(8,128)} %solid_ref.1, s32[16,32,128]{2,1,0:T(8,128)} %ids_ref.1), custom_call_target="tpu_custom_call" | custom-call | tf_op jit(solution)/shard_map/adjoint_steps/pallas_call | solution.py:477
  52.1 2.3 %copy.8 = f32[19,16,32,128]{3,2,1,0:T(8,128)} copy(f32[19,16,32,128]{3,2,1,0:T(8,128)S(1)} %get-tuple-element.2) | data formatting | bytes 9961472
  54.4 0.6 %copy.9 = f32[4,128]{1,0:T(4,128)} copy(f32[4,128]{1,0:T(4,128)S(1)} %get-tuple-element.3) | data formatting | bytes 4096
